TPU v7x, 256 devices: a whole 4x4x8 slice. The times are simulated.
256 devices in a mesh: ctx: 16 (over x_lo, y, core), head: 16 (over z, x_hi).
Axes of the slice: x: 4 (x_hi: 2, x_lo: 2; x = x_hi * 2 + x_lo), y: 4, z: 8, core: 2. Of those that a mesh axis runs over, the one named last changes fastest.
Arguments:
- tokens: bfloat16 [16384, 5376], P('ctx', 'head'), may hold values from -48 to 48
- w_qkv: bfloat16 [5376, 8192], P('ctx', 'head')
Outputs:
- attended: bfloat16 [16384, 4096], P('ctx', 'head')
All inputs are finite; a program needn't handle non-finite values.
Results may differ from a plain program's by a relative error of at most 0.011.
Values may be sent and summed in bfloat16 or wider, within the bound.
No kernel may reach another device: no remote copies, remote signals or barrier semaphores. Data moves between devices by JAX's collectives and lax.ppermute only.
A program may use at most 128 MiB of HBM per device.

v0:
```python
import jax
import jax.numpy as jnp
from jax import lax
from jax.sharding import PartitionSpec as P

HEAD_DIM = 128
Q_PER_KV = 2
WINDOW = 1024
rope_base = 10000.0
query_scale = 168.0 ** (-0.5)
masked_score = -1e30


def passed_along(block, axis, distance):
    devices = range(lax.axis_size(axis))
    route = [(i - distance, i) for i in devices if i - distance in devices]
    return lax.ppermute(block, axis, route)


def rotate(projected, positions):
    head_width = projected.shape[-1]
    half_width = head_width // 2
    inverse = jnp.power(rope_base, -2.0 * jnp.arange(half_width, dtype=jnp.float32) / head_width)
    angles = positions.astype(jnp.float32)[:, None] * inverse[None, :]
    target_shape = (projected.shape[0],) + (1,) * (projected.ndim - 2) + (half_width,)
    cosine = jnp.cos(angles).reshape(target_shape)
    sine_part = jnp.sin(angles).reshape(target_shape)
    leading = projected[..., :half_width]
    second = projected[..., half_width:]
    return jnp.concatenate(
        [leading * cosine - second * sine_part, second * cosine + leading * sine_part], axis=-1
    )


def add_rows(left_rows, shard_rows):
    return jnp.dot(left_rows, shard_rows, preferred_element_type=jnp.float32)


def extend(key_rows, value_rows):
    stacked = jnp.stack([key_rows, value_rows], axis=0)
    border = passed_along(stacked, "ctx", 1)
    return (
        jnp.concatenate([border[0], key_rows], axis=0),
        jnp.concatenate([border[1], value_rows], axis=0),
    )


def attend(queries, key_rows, value_rows, key_anchor):
    row_count = queries.shape[0]
    block_rows = min(512, row_count)
    span = key_rows.shape[0] - row_count
    query_pos = jnp.arange(block_rows, dtype=jnp.int32)[:, None]
    key_pos = jnp.arange(block_rows + span, dtype=jnp.int32)[None, :]

    def one_block(block_index):
        first_row = block_index * block_rows
        query_block = lax.dynamic_slice_in_dim(queries, first_row, block_rows, 0)
        key_block = lax.dynamic_slice_in_dim(key_rows, first_row, block_rows + span, 0)
        value_block = lax.dynamic_slice_in_dim(value_rows, first_row, block_rows + span, 0)
        scores = (
            jnp.einsum("qkgd,ckd->kgqc", query_block, key_block, preferred_element_type=jnp.float32)
            * query_scale
        )
        allowed = (
            (key_pos > query_pos)
            & (key_pos <= query_pos + span)
            & (key_anchor + first_row + key_pos >= 0)
        )
        scores = jnp.where(allowed[None, None], scores, masked_score)
        highest = jnp.max(scores, axis=-1, keepdims=True)
        expanded = jnp.exp(scores - highest)
        probabilities = (expanded / jnp.sum(expanded, axis=-1, keepdims=True)).astype(jnp.bfloat16)
        summed = jnp.einsum(
            "kgqc,ckd->qkgd", probabilities, value_block, preferred_element_type=jnp.float32
        )
        return summed.astype(jnp.bfloat16)

    attended = lax.map(one_block, jnp.arange(row_count // block_rows, dtype=jnp.int32))
    return attended.reshape(row_count, -1)


def on_device(tokens, w_qkv):
    row_count = tokens.shape[0]
    groups = w_qkv.shape[1] // ((Q_PER_KV + 2) * HEAD_DIM)
    device_index = lax.axis_index("ctx")
    positions = device_index * row_count + jnp.arange(row_count, dtype=jnp.int32)
    key_anchor = device_index * row_count - WINDOW
    gathered = lax.all_gather(tokens, "head", axis=1, tiled=True)
    projected = add_rows(gathered, lax.all_gather(w_qkv, "ctx", axis=0, tiled=True))
    projected = projected.reshape(row_count, groups, Q_PER_KV + 2, HEAD_DIM)
    queries = rotate(projected[:, :, :Q_PER_KV], positions).astype(jnp.bfloat16)
    key_rows = rotate(projected[:, :, Q_PER_KV], positions).astype(jnp.bfloat16)
    value_rows = projected[:, :, Q_PER_KV + 1].astype(jnp.bfloat16)
    key_rows, value_rows = extend(key_rows, value_rows)
    return attend(queries, key_rows, value_rows, key_anchor)


def solution(mesh):
    placed = (P("ctx", "head"), P("ctx", "head"))
    return jax.shard_map(
        on_device, mesh=mesh, in_specs=placed, out_specs=P("ctx", "head"), check_vma=False
    )
```

profile of v0, /device:TPU:2, one launch (start us, length us, event | category | flops | bytes accessed | tf_op | source)
XLA Modules:
  0.0 274.9 jit_solution(17137558417569004634)
XLA Ops:
  6.5 0.0 all-gather.5.cloned.1.call-start
  6.5 0.7 all-gather.5.cloned.1.call-update
  7.3 0.0 all-gather.3.cloned.1.call-start
  7.3 0.7 all-gather.3.cloned.1.call-update
  8.1 3.1 %multiply_cosine_fusion = (f32[1024,64]{1,0:T(8,128)}, f32[1024,64]{1,0:T(8,128)}) fusion(f32[64]{0:T(128)S(1)} %multiply_power_fusion, f32[1024]{0:T(1024)S(1)} %add_convert_fusion.1), kind=kLoop, calls=%fused_computation.33 | loop fusion | flops 65536 | bytes 528640 | tf_op jit(solution)/shard_map/cos | solution.py:26
  11.1 43.1 %all-gather.5.cloned.1.call-done = bf16[5376,512]{1,0:T(8,128)(2,1)} async-done(((bf16[336,512]{1,0:T(8,128)(2,1)}), bf16[5376,512]{1,0:T(8,128)(2,1)}) %all-gather.5.cloned.1.call-update) | async-done | bytes 5505040 | tf_op jit(solution)/shard_map/all_gather | solution.py:89
  54.3 164.7 %all-gather.3.cloned.1.call-done = bf16[1024,5376]{0,1:T(8,128)(2,1)} async-done(((bf16[1024,336]{0,1:T(8,128)(2,1)}), bf16[1024,5376]{0,1:T(8,128)(2,1)}) %all-gather.3.cloned.1.call-update) | async-done | bytes 11010064 | tf_op jit(solution)/shard_map/all_gather | solution.py:88
  219.0 10.3 %fusion.37 = f32[1024,512]{0,1:T(8,128)S(1)} fusion(bf16[1024,5376]{0,1:T(8,128)(2,1)} %all-gather.3.cloned.1.call-done, bf16[5376,512]{1,0:T(8,128)(2,1)} %all-gather.5.cloned.1.call-done), kind=kOutput, calls=%fused_computation.56 | convolution fusion | flops 5637144576 | bytes 18612224 | tf_op jit(solution)/shard_map/dot_general | solution.py:36
  229.3 0.0 copy-start
  229.4 1.3 copy-done
  230.7 0.2 copy.21
  230.9 2.4 fusion.33
  233.3 0.2 copy.22
  233.5 1.0 pad_maximum_fusion
  234.4 2.1 collective-permute-start
  236.5 1.3 fusion.36
  237.8 0.3 copy.23
  238.1 0.3 copy.24
  238.5 1.5 subtract_convert_fusion
  240.0 0.3 pad_maximum_fusion.2
  240.3 7.1 %collective-permute-done = bf16[2,1024,1,128]{3,1,2,0:T(8,128)(2,1)} collective-permute-done((bf16[2,1024,1,128]{3,1,2,0:T(8,128)(2,1)}, bf16[2,1024,1,128]{3,1,2,0:T(8,128)(2,1)}, u32[]{:S(2)}, u32[]{:S(2)}) %collective-permute-start) | collective-permute-done | bytes 524320 | tf_op jit(solution)/shard_map/ppermute | solution.py:17
  247.3 1.1 slice_bitcast_fusion
  248.4 0.2 pad_maximum_fusion.1
  248.6 17.6 %while.12 = (s32[]{:T(128)}, bf16[2,512,1,2,128]{4,3,1,0,2:T(2,128)(2,1)}, s32[2]{0:T(128)S(1)}, bf16[2048,1,128]{2,0,1:T(8,128)(2,1)S(1)}, s32[]{:T(128)}, /*in...) while((s32[]{:T(128)}, ...), condition=%wide.region_3.4_spmd.clone.clone, body=%wide.region_0.3_spmd.clone.clone.sunk | while | flops 827459072 | bytes 28601632 | solution.py:78
  248.6 0.6 dynamic_slice.44
  249.9 1.3 fusion.50
  251.1 1.4 fusion.51
  252.5 1.4 fusion.52
  254.0 0.0 copy-start.1
  254.0 2.2 fusion.53
  256.2 0.2 copy.29
  256.3 0.0 copy-done.1
  256.4 0.2 constant_dynamic-update-slice_fusion.2
  256.6 0.0 copy-start.2
  256.6 0.8 copy-done.2
  257.4 0.6 dynamic_slice.44
  258.6 1.3 fusion.50
  259.9 1.4 fusion.51
  261.3 1.4 fusion.52
  262.7 0.0 copy-start.1
  262.8 2.2 fusion.53
  264.9 0.2 copy.29
  265.1 0.0 copy-done.1
  265.1 0.2 constant_dynamic-update-slice_fusion.2
  265.3 0.0 copy-start.2
  265.4 0.8 copy-done.2
  266.1 1.9 copy.27
  (10 shorter events, 0.1 us)
Async XLA Ops:
  6.5 47.7 %all-gather.5.cloned.1.call-start = ((), (), s32[]{:S(2)}) async-start(), calls=%async_computation.1 | async-start | bytes 5849088 | tf_op jit(solution)/shard_map/all_gather | solution.py:89
  7.3 211.7 %all-gather.3.cloned.1.call-start = ((), (), s32[]{:S(2)}) async-start(), calls=%async_computation | async-start | bytes 11698176 | tf_op jit(solution)/shard_map/all_gather | solution.py:88
  229.3 1.3 copy-start
  234.4 12.9 %collective-permute-start = (bf16[2,1024,1,128]{3,1,2,0:T(8,128)(2,1)}, bf16[2,1024,1,128]{3,1,2,0:T(8,128)(2,1)}, u32[]{:S(2)}, u32[]{:S(2)}) collective-permute-start(bf16[2,1024,1,128]{3,1,2,0:T(8,128)(2,1)} %pad_maximum_fusion), channel_id=1, source_target_pairs={{0,16},{16,32},{32,48},{48,64},{64,80},{80,96},{96,112},{112,128},... | collective-permute-start | bytes 1572872 | tf_op jit(solution)/shard_map/ppermute | solution.py:17
  254.0 2.4 copy-start.1
  256.6 0.8 copy-start.2
  262.7 2.4 copy-start.1
  265.3 0.8 copy-start.2
Sparse Core Ops, SparseCore 0:
  9.2 45.0 all-gather.4
  56.9 162.0 all-gather.2
where the time goes:
time: 275 us
  waiting for transfers between devices  216 us (79%)
  matrix products  17.5 us (6%)
  other arithmetic  13.8 us (5%)
  between operations  13.5 us (5%)
  local copies, waits for them, and re-layouts  10.1 us (4%)
    all_gather x1, waiting for transfers between devices, on_device(): gathered = lax.all_gather(tokens, 'head', axis=1, tiled=True)  165 us
    all_gather x1, waiting for transfers between devices, on_device(): lax.all_gather(w_qkv, 'ctx', axis=0, tiled=True)  43.1 us
    dot_general x1, matrix products, add_rows(): return jnp.dot(left_rows, shard_rows, preferred_element_type=jnp.float32)  10.3 us
    ppermute x1, waiting for transfers between devices, passed_along(): return lax.ppermute(block, axis, route)  7.08 us
  transfers between devices with their start and end apart: 3, of which 3 were waited for; matrix products, arithmetic and copies ran while one was open for 2% of the time, Pallas kernels for 0%

commit v1 on v0

--- a/solution.py
+++ b/solution.py
@@ -86,7 +86,12 @@
     positions = device_index * row_count + jnp.arange(row_count, dtype=jnp.int32)
     key_anchor = device_index * row_count - WINDOW
     gathered = lax.all_gather(tokens, "head", axis=1, tiled=True)
-    projected = add_rows(gathered, lax.all_gather(w_qkv, "ctx", axis=0, tiled=True))
+    projected = add_rows(
+        gathered,
+        jnp.concatenate(
+            lax.all_to_all(jnp.stack([w_qkv] * lax.axis_size("ctx")), "ctx", 0, 0), axis=0
+        ),
+    )
     projected = projected.reshape(row_count, groups, Q_PER_KV + 2, HEAD_DIM)
     queries = rotate(projected[:, :, :Q_PER_KV], positions).astype(jnp.bfloat16)
     key_rows = rotate(projected[:, :, Q_PER_KV], positions).astype(jnp.bfloat16)

time: 275 us -> 248 us (0.902)
  waiting for transfers between devices: 216 us -> 181 us
  starting transfers between devices: 2.13 us -> 8.6 us
  other arithmetic: 13.8 us -> 7.92 us
  local copies, waits for them, and re-layouts: 10.1 us -> 15 us
    all_to_all x0 -> x1, waiting for transfers between devices: none -> 87 us  [on_device(): lax.all_to_all(jnp.stack([w_qkv] * lax.axis_size('ctx')), 'ctx', 0, 0)]
    all_gather x1, waiting for transfers between devices: 165 us -> 84 us  [on_device(): gathered = lax.all_gather(tokens, 'head', axis=1, tiled=True)]
    all_gather x1 -> x0, waiting for transfers between devices: 43.1 us -> none  [on_device(): lax.all_gather(w_qkv, 'ctx', axis=0, tiled=True)]
    dot_general x0 -> x1, local copies, waits for them, and re-layouts: none -> 8.02 us  [add_rows(): return jnp.dot(left_rows, shard_rows, preferred_element_type=jnp.float32)]
    all_to_all x0 -> x1, starting transfers between devices: none -> 6.68 us  [on_device(): lax.all_to_all(jnp.stack([w_qkv] * lax.axis_size('ctx')), 'ctx', 0, 0)]
    another operation x0 -> x1, local copies, waits for them, and re-layouts: none -> 3.89 us  [on_device(): jnp.stack([w_qkv] * lax.axis_size('ctx'))]
    unnamed x7 -> x1, local copies, waits for them, and re-layouts: 4.22 us -> 0.88 us
  transfers between devices with their start and end apart: 3 -> 3, of which waited for: 3 -> 3; matrix products, arithmetic and copies ran while one was open for 2% -> 5% of each run, Pallas kernels for 0% -> 0%
where the time goes in v1:
time: 248 us; the launch traced here: 245 us
  waiting for transfers between devices  181 us (73%)
  matrix products  17.6 us (7%)
  local copies, waits for them, and re-layouts  15 us (6%)
  between operations  13.5 us (5%)
  starting transfers between devices  8.6 us (3%)
  other arithmetic  7.92 us (3%)
    all_to_all x1, waiting for transfers between devices, on_device(): lax.all_to_all(jnp.stack([w_qkv] * lax.axis_size('ctx')), 'ctx', 0, 0)  87 us
    all_gather x1, waiting for transfers between devices, on_device(): gathered = lax.all_gather(tokens, 'head', axis=1, tiled=True)  84 us
    dot_general x1, matrix products, add_rows(): return jnp.dot(left_rows, shard_rows, preferred_element_type=jnp.float32)  10.3 us
    ppermute x1, waiting for transfers between devices, passed_along(): return lax.ppermute(block, axis, route)  9.46 us
    dot_general x1, local copies, waits for them, and re-layouts, add_rows(): return jnp.dot(left_rows, shard_rows, preferred_element_type=jnp.float32)  8.02 us
    all_to_all x1, starting transfers between devices, on_device(): lax.all_to_all(jnp.stack([w_qkv] * lax.axis_size('ctx')), 'ctx', 0, 0)  6.68 us
  transfers between devices with their start and end apart: 3, of which 3 were waited for; matrix products, arithmetic and copies ran while one was open for 5% of the time, Pallas kernels for 0%

profile of v1, /device:TPU:2, one launch (start us, length us, event | category | flops | bytes accessed | tf_op | source)
XLA Modules:
  0.0 245.3 jit_solution(4412483296459010649)
XLA Ops:
  6.5 0.0 all-gather.2.cloned.1.call-start
  6.5 0.7 all-gather.2.cloned.1.call-update
  7.3 3.9 %stack.4 = bf16[16,336,512]{2,1,0:T(8,128)(2,1)} broadcast(bf16[336,512]{1,0:T(8,128)(2,1)} %param.5), dimensions={1,2} | broadcast | bytes 5849088 | tf_op jit(solution)/shard_map/stack | solution.py:92
  11.1 6.7 %all-to-all-start = ((bf16[16,336,512]{2,1,0:T(8,128)(2,1)}), bf16[16,336,512]{2,1,0:T(8,128)(2,1)}, u32[]{:S(2)}, u32[]{:S(2)}) async-start(bf16[16,336,512]{2,1,0:T(8,128)(2,1)} %stack.4), calls=%async_computation | async-start | bytes 11010048 | tf_op jit(solution)/shard_map/all_to_all | solution.py:92
  17.9 87.0 %all-to-all-done = bf16[16,336,512]{2,1,0:T(8,128)(2,1)} async-done(((bf16[16,336,512]{2,1,0:T(8,128)(2,1)}), bf16[16,336,512]{2,1,0:T(8,128)(2,1)}, u32[]{:S(2)}, u32[]{:S(2)}) %all-to-all-start) | async-done | bytes 5505056 | tf_op jit(solution)/shard_map/all_to_all | solution.py:92
  104.9 8.0 %copy.9 = bf16[512,5376]{1,0:T(8,128)(2,1)} copy(bf16[512,5376]{0,1:T(8,128)(2,1)} %bitcast.2) | data formatting | bytes 11010048 | tf_op jit(solution)/shard_map/dot_general | solution.py:36
  112.9 84.0 %all-gather.2.cloned.1.call-done = bf16[1024,5376]{0,1:T(8,128)(2,1)} async-done(((bf16[1024,336]{0,1:T(8,128)(2,1)}), bf16[1024,5376]{0,1:T(8,128)(2,1)}) %all-gather.2.cloned.1.call-update) | async-done | bytes 11010064 | tf_op jit(solution)/shard_map/all_gather | solution.py:88
  196.9 10.3 %fusion.30 = f32[1024,1,4,128]{0,3,2,1:T(8,128)S(1)} fusion(bf16[4,128,5376]{2,1,0:T(8,128)(2,1)} %bitcast.96, bf16[1024,5376]{0,1:T(8,128)(2,1)} %all-gather.2.cloned.1.call-done), kind=kOutput, calls=%fused_computation.32 | convolution fusion | flops 5637144576 | bytes 18612224 | tf_op jit(solution)/shard_map/dot_general | solution.py:36
  207.3 1.2 fusion.38
  208.5 1.9 collective-permute-start
  210.4 1.0 multiply_cosine_fusion
  211.4 0.2 subtract_convert_fusion
  211.6 9.5 %collective-permute-done = bf16[2,1024,1,128]{1,3,2,0:T(8,128)(2,1)S(1)} collective-permute-done((bf16[2,1024,1,128]{1,3,2,0:T(8,128)(2,1)S(1)}, bf16[2,1024,1,128]{1,3,2,0:T(8,128)(2,1)S(1)}, u32[]{:S(2)}, u32[]{:S(2)}) %collective-permute-start) | collective-permute-done | bytes 524320 | tf_op jit(solution)/shard_map/ppermute | solution.py:17
  221.1 0.1 pad_maximum_fusion.1
  221.2 16.3 %while.12 = (s32[]{:T(128)}, bf16[2,512,1,2,128]{4,3,1,0,2:T(2,128)(2,1)S(1)}, s32[2]{0:T(128)S(1)}, bf16[2048,1,128]{0,2,1:T(8,128)(2,1)S(1)}, s32[]{:T(128)}, ...) while((s32[]{:T(128)}, ...), condition=%wide.region_3.4_spmd.clone.clone, body=%wide.region_0.3_spmd.clone.clone.sunk | while | flops 827459072 | bytes 24407272 | solution.py:78
  221.3 0.7 dynamic_slice.44
  222.6 1.3 fusion.54
  223.9 1.5 fusion.55
  225.4 1.4 fusion.56
  226.8 2.2 fusion.57
  229.0 0.2 copy.22
  229.2 0.2 constant_dynamic-update-slice_fusion.2
  229.4 0.7 dynamic_slice.44
  230.8 1.3 fusion.54
  232.0 1.5 fusion.55
  233.5 1.4 fusion.56
  235.0 2.2 fusion.57
  237.1 0.2 copy.22
  237.3 0.2 constant_dynamic-update-slice_fusion.2
  237.5 0.9 copy.20
  (13 shorter events, 0.2 us)
Async XLA Ops:
  6.5 190.3 %all-gather.2.cloned.1.call-start = ((), (), s32[]{:S(2)}) async-start(), calls=%async_computation.1 | async-start | bytes 11698176 | tf_op jit(solution)/shard_map/all_gather | solution.py:88
  11.1 93.7 %all-to-all-start = ((bf16[16,336,512]{2,1,0:T(8,128)(2,1)}), bf16[16,336,512]{2,1,0:T(8,128)(2,1)}, u32[]{:S(2)}, u32[]{:S(2)}) async-start(bf16[16,336,512]{2,1,0:T(8,128)(2,1)} %stack.4), calls=%async_computation | async-start | bytes 11010048 | tf_op jit(solution)/shard_map/all_to_all | solution.py:92
  208.5 12.6 %collective-permute-start = (bf16[2,1024,1,128]{1,3,2,0:T(8,128)(2,1)S(1)}, bf16[2,1024,1,128]{1,3,2,0:T(8,128)(2,1)S(1)}, u32[]{:S(2)}, u32[]{:S(2)}) collective-permute-start(bf16[2,1024,1,128]{1,3,2,0:T(8,128)(2,1)S(1)} %pad_maximum_fusion), channel_id=1, source_target_pairs={{0,16},{16,32},{32,48},{48,64},{64,80},{80,96},{96,112},{112,128},... | collective-permute-start | bytes 1572872 | tf_op jit(solution)/shard_map/ppermute | solution.py:17
Sparse Core Ops, SparseCore 0:
  9.9 186.8 all-gather.1
